TPU v7x, 512 devices: a whole 4x4x16 slice. The times are simulated.
512 devices in a mesh: dp: 16 (over y, z_hi, core), fsdp: 32 (over x, z_lo).
Axes of the slice: x: 4, y: 4, z: 16 (z_hi: 2, z_lo: 8; z = z_hi * 8 + z_lo), core: 2. Of those that a mesh axis runs over, the one named last changes fastest.
Arguments:
- activations: bfloat16 [1024, 8192], P('fsdp', 'dp'), may hold values from -6 to 6
- cotangents: bfloat16 [1024, 8192], P('fsdp', 'dp'), may hold values from -6 to 6
- gate_weight: bfloat16 [8192, 14336], P('dp', 'fsdp'), may hold values from -0.0625 to 0.0625
- down_weight: bfloat16 [14336, 8192], P('fsdp', 'dp'), may hold values from -0.046875 to 0.046875
- query_grads: bfloat16 [8, 8192, 14336], P(None, 'dp', 'fsdp'), may hold values from -0.0012207031 to 0.0012207031
Outputs:
- scores: float32 [1024, 8], P(('dp', 'fsdp'))
All inputs are finite; a program needn't handle non-finite values.
Results may differ from a plain program's by a relative error of at most 0.0075.
Values may be sent and summed in bfloat16 or wider, within the bound.
A program may use at most 64 MiB of HBM per device.

v0:
```python
import jax
import jax.numpy as jnp
from jax import lax
from jax.sharding import PartitionSpec as P


def per_device(activations, cotangents, gate_weight, down_weight, query_grads):
    gathered = lax.all_gather(activations, "fsdp", axis=0, tiled=True)
    back_partial = lax.dot_general(
        lax.all_gather(cotangents, "fsdp", axis=0, tiled=True),
        down_weight,
        (((1,), (1,)), ((), ())),
        preferred_element_type=jnp.float32,
    )
    tokens = gathered.shape[0]
    gate_partial = jnp.dot(gathered, gate_weight, preferred_element_type=jnp.float32)
    gate_sum, back_sum = lax.psum((gate_partial, back_partial), "dp")
    signal = (jax.nn.silu(gate_sum) * back_sum).astype(jnp.bfloat16)
    block_rows = 512
    queries_count = query_grads.shape[0]

    def score_block(number):
        act_rows = lax.dynamic_slice_in_dim(gathered, number * block_rows, block_rows, 0)
        signal_rows = lax.dynamic_slice_in_dim(signal, number * block_rows, block_rows, 0)
        projected = jnp.einsum(
            "ti,qij->tqj", act_rows, query_grads, preferred_element_type=jnp.float32
        )
        return jnp.sum(projected * signal_rows.astype(jnp.float32)[:, None, :], axis=2)

    partial_scores = lax.map(score_block, jnp.arange(tokens // block_rows, dtype=jnp.int32))
    partial_scores = partial_scores.reshape(tokens, queries_count)
    scores = lax.psum_scatter(partial_scores, ("dp", "fsdp"), scatter_dimension=0, tiled=True)
    return scores


def solution(mesh):
    placed = (
        P("fsdp", "dp"),
        P("fsdp", "dp"),
        P("dp", "fsdp"),
        P("fsdp", "dp"),
        P(None, "dp", "fsdp"),
    )
    return jax.shard_map(
        per_device, mesh=mesh, in_specs=placed, out_specs=P(("dp", "fsdp"), None), check_vma=False
    )
```

profile of v0, /device:TPU:1, one launch (start us, length us, event | category | flops | bytes accessed | tf_op | source)
XLA Modules:
  0.0 975.3 jit_solution(8148526495166351739)
XLA Ops:
  6.5 0.0 copy-start
  6.5 0.0 all-gather.3.cloned.1.call-start
  6.5 0.7 all-gather.3.cloned.1.call-update
  7.3 0.0 all-gather.5.cloned.1.call-start
  7.3 0.7 all-gather.5.cloned.1.call-update
  8.0 0.0 all-reduce.4.cloned.1.call-start
  8.1 207.7 %all-gather.3.cloned.1.call-done = bf16[1024,512]{1,0:T(8,128)(2,1)} async-done(((bf16[32,512]{1,0:T(8,128)(2,1)}), bf16[1024,512]{1,0:T(8,128)(2,1)}) %all-gather.3.cloned.1.call-update) | async-done | bytes 1048592 | tf_op jit(solution)/shard_map/all_gather | solution.py:8
  215.7 3.1 fusion.3
  218.9 219.6 %all-gather.5.cloned.1.call-done = bf16[1024,512]{1,0:T(8,128)(2,1)} async-done(((bf16[32,512]{1,0:T(8,128)(2,1)}), bf16[1024,512]{1,0:T(8,128)(2,1)}) %all-gather.5.cloned.1.call-update) | async-done | bytes 1048592 | tf_op jit(solution)/shard_map/all_gather | solution.py:10
  438.5 0.0 copy-done.2
  438.5 3.1 fusion.4
  441.6 0.0 all-reduce.4.cloned.1.call-update
  441.7 401.5 %all-reduce.4.cloned.1.call-done = (f32[1024,448]{0,1:T(8,128)}, f32[1024,448]{0,1:T(8,128)}) async-done(((f32[1024,448]{0,1:T(8,128)}, f32[1024,448]{0,1:T(8,128)}), (f32[1024,448]{0,1:T(8,128)}, f32[1024,448]{0,1:T(8,128)})) %all-reduce.4.cloned.1.call-update) | async-done | bytes 3670032 | tf_op jit(solution)/shard_map/psum | solution.py:17
  843.2 2.7 multiply_convert_fusion
  845.9 11.3 %while.10 = (s32[]{:T(128)}, f32[2,512,8]{1,2,0:T(8,128)S(1)}, s32[2]{0:T(128)S(1)}, bf16[1024,512]{1,0:T(8,128)(2,1)S(1)}, bf16[8,512,448]{1,2,0:T(8,128)(2,1)}...) while((s32[]{:T(128)}, f32[2,512,8]{1,2,0:T(8,128)S(1)}, ...), condition=%wide.region_4.5_spmd, body=%wide.region_2.4_spmd.sunk | while | flops 1882943488 | bytes 6537387 | solution.py:30
  845.9 0.7 dynamic_slice.20
  847.2 0.1 dynamic-slice_convert_fusion.2
  847.3 4.2 multiply_reduce_fusion.2
  851.5 0.7 dynamic_slice.20
  852.9 0.1 dynamic-slice_convert_fusion.2
  853.0 4.2 multiply_reduce_fusion.2
  857.2 0.2 copy.7
  857.4 110.8 %all-reduce = f32[1024,8]{1,0:T(8,128)S(1)} all-reduce(f32[1024,8]{1,0:T(8,128)S(1)} %bitcast.20), channel_id=2, replica_groups=mesh['dp'=16,'fsdp'=32] {'dp','fsdp'}, use_global_device_ids=true, to_apply=%region_5.6.clone | all-reduce | flops 8192 | bytes 65536
  968.2 0.6 constant_dynamic-slice_fusion
  (8 shorter events, 0.0 us)
Async XLA Ops:
  6.5 209.2 %copy-start = (bf16[512,448]{0,1:T(8,128)(2,1)S(1)}, bf16[512,448]{0,1:T(8,128)(2,1)}, u32[]{:S(2)}) copy-start(bf16[512,448]{0,1:T(8,128)(2,1)} %param.9) | copy-start | bytes 1376260
  6.5 432.0 %copy-start.2 = (bf16[448,512]{1,0:T(8,128)(2,1)S(1)}, bf16[448,512]{1,0:T(8,128)(2,1)}, u32[]{:S(2)}) copy-start(bf16[448,512]{1,0:T(8,128)(2,1)} %param.10) | copy-start | bytes 1376260
  6.5 209.2 %all-gather.3.cloned.1.call-start = ((), (), s32[]{:S(2)}) async-start(), calls=%async_computation | async-start | bytes 1081344 | tf_op jit(solution)/shard_map/all_gather | solution.py:8
  7.3 431.2 %all-gather.5.cloned.1.call-start = ((), (), s32[]{:S(2)}) async-start(), calls=%async_computation.1 | async-start | bytes 1081344 | tf_op jit(solution)/shard_map/all_gather | solution.py:10
  8.0 835.1 %all-reduce.4.cloned.1.call-start = ((), (), s32[]{:S(2)}) async-start(), calls=%async_computation.2 | async-start | bytes 7340032 | tf_op jit(solution)/shard_map/psum | solution.py:17
  843.2 2.7 copy-start.1
Sparse Core Ops, SparseCore 0:
  9.4 206.2 all-gather.2
  217.8 220.6 all-gather.4
  441.8 401.3 all-reduce.3
where the time goes:
time: 976 us; the launch traced here: 975 us
  waiting for transfers between devices  830 us (85%)
  blocking collectives  111 us (11%)
  matrix products  14.6 us (1%)
  between operations  13.2 us (1%)
    psum x1, waiting for transfers between devices, per_device(): gate_sum, back_sum = lax.psum((gate_partial, back_partial), 'dp')  401 us
    all_gather x1, waiting for transfers between devices, per_device(): lax.all_gather(cotangents, 'fsdp', axis=0, tiled=True)  220 us
    all_gather x1, waiting for transfers between devices, per_device(): gathered = lax.all_gather(activations, 'fsdp', axis=0, tiled=True)  208 us
    unnamed x1, blocking collectives  111 us
  transfers between devices with their start and end apart: 3, of which 3 were waited for; matrix products, arithmetic and copies ran while one was open for 0% of the time, Pallas kernels for 0%

commit v1 on v0

v1 whole, which is shorter than its diff:
```python
import functools

import jax
import jax.numpy as jnp
from jax import lax
from jax.experimental import pallas as pl
from jax.experimental.pallas import tpu as pltpu
from jax.sharding import PartitionSpec as P

MESH = pl.DeviceIdType.MESH
F32 = jnp.float32
BF16 = jnp.bfloat16
NY, NH, NC, NX, NZ = 4, 2, 2, 4, 8
CHUNKS = 4
WHOLE_H = (False, False, False, True)


def nearest(z, i):
    reach = jnp.minimum(z, NZ - 1 - z)
    inner = z - (i + 1) // 2 if i % 2 else z + i // 2
    outer = jnp.where(z < NZ // 2, i, NZ - 1 - i)
    return jnp.where(i <= 2 * reach, inner, outer)


def kernel(
    act, cot, gate_w, down_w, query, out,
    ag, gw, dw, qt, qg, actt,
    c_out, c_in, acc, y_out, y_in, acc2, h_out, h_in, sig,
    scores, f1_in, f1_acc, f2_in, f2_acc, f3_in,
    load, z_s, z_r, x_s, x_r, w_s, w_r,
    c_s, c_r, y_s, y_r, h_s, h_r, hs_s, hs_r, ys_s, ys_r, cs_s, cs_r,
    f1_s, f1_r, f2_s, f2_r, f3_s, f3_r,
):
    p, f = lax.axis_index("dp"), lax.axis_index("fsdp")
    y, h, c = p // 4, (p // 2) % 2, p % 2
    x, z = f // NZ, f % NZ

    def dev(dy=0, dh=0, dc=0, dx=0, dz=0):
        ty, th, tc = (y + dy) % NY, (h + dh) % NH, (c + dc) % NC
        tx, tz = (x + dx) % NX, z + dz
        return (ty * 4 + th * 2 + tc, tx * NZ + tz)

    rows, width = act.shape
    slab = NX * rows
    part, half = slab // NY, slab // NY // NH
    queries = query.shape[0]

    mine = pl.ds(pl.multiple_of(x * rows, rows), rows)
    loads = [
        pltpu.make_async_copy(act, ag.at[0, z, mine], load.at[0]),
        pltpu.make_async_copy(cot, ag.at[1, z, mine], load.at[1]),
        pltpu.make_async_copy(gate_w, gw, load.at[2]),
        pltpu.make_async_copy(down_w, dw, load.at[3]),
        pltpu.make_async_copy(query, qt, load.at[4]),
    ]
    for item in loads:
        item.start()

    barrier = pltpu.get_barrier_semaphore()

    def greet(device):
        pl.semaphore_signal(barrier, inc=1, device_id=device, device_id_type=MESH)

    greet(dev(dx=1))
    greet(dev(dx=3))
    pl.when(z > 0)(lambda: greet(dev(dz=-1)))
    pl.when(z < NZ - 1)(lambda: greet(dev(dz=1)))
    greet(dev(dc=1))
    for dy in range(1, NY):
        greet(dev(dy=dy))
    greet(dev(dh=1))
    loads[0].wait()
    loads[1].wait()
    line = jnp.where(z > 0, 1, 0) + jnp.where(z < NZ - 1, 1, 0)
    pl.semaphore_wait(barrier, line + 7)

    def remote(src, dst, send, recv, device):
        return pltpu.make_async_remote_copy(
            src_ref=src, dst_ref=dst, send_sem=send, recv_sem=recv,
            device_id=device, device_id_type=MESH,
        )

    sides = [(s, d) for s in range(NZ) for d in range(2) if s or not d]

    def valid(s, d):
        return z >= s if d == 0 else z + s <= NZ - 1

    def at_z(s, d):
        return jnp.clip(z - s if d == 0 else z + s, 0, NZ - 1)

    def spot(zz, xx):
        return (zz, pl.ds(pl.multiple_of(xx * rows, rows), rows))

    def z_copy(s, d):
        where = spot(at_z(s - 1, d), x)
        block = ag.at[:, where[0], where[1]]
        return remote(block, block, z_s.at[d, s], z_r.at[d, s], dev(dz=1 - 2 * d))

    def z_land(s, d):
        where = spot(at_z(s, d), x)
        block = ag.at[:, where[0], where[1]]
        return remote(block, block, z_s.at[d, s], z_r.at[d, s], dev(dz=2 * d - 1))

    def x_copy(s, d, e):
        where = spot(at_z(s, d), x)
        block = ag.at[:, where[0], where[1]]
        k = 2 * s + d
        return remote(block, block, x_s.at[e, k], x_r.at[e, k], dev(dx=1 + 2 * e))

    def x_land(s, d, e):
        where = spot(at_z(s, d), (x + 3 - 2 * e) % NX)
        block = ag.at[:, where[0], where[1]]
        k = 2 * s + d
        return remote(block, block, x_s.at[e, k], x_r.at[e, k], dev(dx=3 - 2 * e))

    def w_copy(s, d, e):
        where = spot(at_z(s, d), (x + 3 - 2 * e) % NX)
        block = ag.at[e, where[0], where[1]]
        k = 2 * s + d
        return remote(block, block, w_s.at[e, k], w_r.at[e, k], dev(dx=1 + 2 * e))

    def w_land(s, d, e):
        where = spot(at_z(s, d), (x + 2) % NX)
        block = ag.at[e, where[0], where[1]]
        k = 2 * s + d
        return remote(block, block, w_s.at[e, k], w_r.at[e, k], dev(dx=3 - 2 * e))

    def ds_of(s):
        return (0,) if s == 0 else (0, 1)

    def step_z(s):
        for d in ds_of(s):
            def body(d=d):
                if s:
                    z_land(s, d).wait_recv()
                if s < NZ - 1:
                    if s:
                        pl.when(z < NZ - 1 if d == 0 else z > 0)(lambda: z_copy(s + 1, d).start())
                    else:
                        pl.when(z < NZ - 1)(lambda: z_copy(1, 0).start())
                        pl.when(z > 0)(lambda: z_copy(1, 1).start())
                x_copy(s, d, 0).start()
                x_copy(s, d, 1).start()
            pl.when(valid(s, d))(body)

    def step_x(s):
        for d in ds_of(s):
            def body(d=d):
                for e in range(2):
                    x_land(s, d, e).wait_recv()
                    w_copy(s, d, e).start()
            pl.when(valid(s, d))(body)

    def step_w(s):
        for d in ds_of(s):
            def body(d=d):
                for e in range(2):
                    w_land(s, d, e).wait_recv()
            pl.when(valid(s, d))(body)

    def drain_gather():
        for s, d in sides:
            if s:
                going = (z >= s - 1) & (z < NZ - 1) if d == 0 else (z + s - 1 <= NZ - 1) & (z > 0)
                pl.when(going)(lambda s=s, d=d: z_copy(s, d).wait_send())

            def body(s=s, d=d):
                for e in range(2):
                    x_copy(s, d, e).wait_send()
                    w_copy(s, d, e).wait_send()
            pl.when(valid(s, d))(body)

    def turn_queries(first, count):
        def one(q, carry):
            qg[q] = qt[q].T
            return carry

        lax.fori_loop(first, first + count, one, 0)

    def products(zz, store):
        for n, weight in enumerate((gw, dw)):
            store(n, lax.dot_general(
                ag[n, zz], weight[...], (((1,), (1,)), ((), ())), preferred_element_type=F32
            ))

    def slab_of(k, core):
        first, second = nearest(z, 2 * k), nearest(z, 2 * k + 1)
        return jnp.where(core == 0, first, second)

    def c_copy(k):
        return remote(c_out.at[k], c_in.at[k], c_s.at[k], c_r.at[k], dev(dc=1))

    def stage_products(k):
        def to_peer(n, value):
            c_out[k, n] = value.astype(BF16)

        def to_own(n, value):
            acc[k, n] = value

        products(slab_of(k, 1 - c), to_peer)
        c_copy(k).start()
        products(slab_of(k, c), to_own)

    def y_rows(yy):
        return pl.ds(pl.multiple_of(yy * part, part), part)

    def y_copy(k, dy):
        return remote(
            y_out.at[k, :, y_rows((y + dy) % NY)], y_in.at[k, dy - 1],
            y_s.at[k, dy - 1], y_r.at[k, dy - 1], dev(dy=dy),
        )

    def stage_core(k):
        c_copy(k).wait_recv()
        total = acc[k] + c_in[k].astype(F32)
        acc[k] = total
        y_out[k] = total.astype(BF16)
        for dy in (2, 1, 3):
            y_copy(k, dy).start()

    def h_rows(hh):
        return pl.ds(pl.multiple_of(hh * half, half), half)

    def h_copy(k):
        if WHOLE_H[k]:
            return remote(h_out.at[k], h_in.at[k], h_s.at[k], h_r.at[k], dev(dh=1))
        return remote(
            h_out.at[k, :, h_rows(1 - h)], h_in.at[k, :, pl.ds(0, half)],
            h_s.at[k], h_r.at[k], dev(dh=1),
        )

    def stage_y(k):
        total = acc[k, :, y_rows(y)]
        for dy in range(1, NY):
            y_copy(k, dy).wait_recv()
            total = total + y_in[k, dy - 1].astype(F32)
        acc2[k] = total
        h_out[k] = total.astype(BF16)
        h_copy(k).start()

    def s_rows(yy, hh):
        return pl.ds(pl.multiple_of(yy * part + hh * half, half), half)

    def hs_copy(k):
        block = sig.at[k, c, s_rows(y, h)]
        return remote(block, block, hs_s.at[k], hs_r.at[k], dev(dh=1))

    def hs_land(k):
        block = sig.at[k, c, s_rows(y, 1 - h)]
        return remote(block, block, hs_s.at[k], hs_r.at[k], dev(dh=1))

    def ys_copy(k, dy):
        block = sig.at[k, c, y_rows(y)]
        return remote(block, block, ys_s.at[k, dy - 1], ys_r.at[k, dy - 1], dev(dy=dy))

    def ys_land(k, dy):
        block = sig.at[k, c, y_rows((y + NY - dy) % NY)]
        return remote(block, block, ys_s.at[k, dy - 1], ys_r.at[k, dy - 1], dev(dy=dy))

    def cs_copy(k):
        block = sig.at[k, c]
        return remote(block, block, cs_s.at[k], cs_r.at[k], dev(dc=1))

    def cs_land(k):
        block = sig.at[k, 1 - c]
        return remote(block, block, cs_s.at[k], cs_r.at[k], dev(dc=1))

    def signal_of(total):
        gate, back = total[0], total[1]
        return (gate / (1.0 + jnp.exp(-gate)) * back).astype(BF16)

    def stage_h(k):
        h_copy(k).wait_recv()
        if WHOLE_H[k]:
            sig[k, c, y_rows(y)] = signal_of(acc2[k] + h_in[k].astype(F32))
            for dy in (2, 1, 3):
                ys_copy(k, dy).start()
        else:
            total = acc2[k, :, h_rows(h)] + h_in[k, :, pl.ds(0, half)].astype(F32)
            sig[k, c, s_rows(y, h)] = signal_of(total)
            hs_copy(k).start()

    def stage_hs(k):
        if not WHOLE_H[k]:
            hs_land(k).wait_recv()
            for dy in (2, 1, 3):
                ys_copy(k, dy).start()

    def stage_ys(k):
        for dy in range(1, NY):
            ys_land(k, dy).wait_recv()
        cs_copy(k).start()

    def turn(k):
        for n in range(2):
            actt[k, :, n * slab:(n + 1) * slab] = ag[0, nearest(z, 2 * k + n)].astype(F32).T

    def stage_scores(k):
        cs_land(k).wait_recv()
        both = sig[k].reshape(2 * slab, sig.shape[-1])
        first, second = nearest(z, 2 * k), nearest(z, 2 * k + 1)

        def one(q, carry):
            back = lax.dot_general(
                qg[q], both, (((1,), (1,)), ((), ())), preferred_element_type=F32
            )
            line = jnp.sum(back * actt[k], axis=0, keepdims=True)
            scores[first, pl.ds(q, 1), :] = line[:, :slab]
            scores[second, pl.ds(q, 1), :] = line[:, slab:]
            return carry

        lax.fori_loop(0, queries, one, 0)

    def drain_chunk(k):
        c_copy(k).wait_send()
        h_copy(k).wait_send()
        if not WHOLE_H[k]:
            hs_copy(k).wait_send()
        for dy in range(1, NY):
            y_copy(k, dy).wait_send()
            ys_copy(k, dy).wait_send()
        cs_copy(k).wait_send()

    for step in range(NZ + 2):
        if step < NZ:
            step_z(step)
        if 1 <= step < NZ + 1:
            step_x(step - 1)
        if step >= 2:
            step_w(step - 2)
        if step == 0:
            loads[4].wait()
        if step < 4:
            turn_queries(2 * step, 2)
        if step == 2:
            loads[2].wait()
            loads[3].wait()
        ready = step - 2
        if ready >= 1 and ready % 2 == 1:
            k = ready // 2
            stage_products(k)
            turn(k)
        if ready >= 1:
            k = (ready - 1) // 2
            if ready % 2 == 0:
                stage_core(k)
            elif k >= 1:
                stage_y(k - 1)
    last = CHUNKS - 1
    stage_core(last)
    stage_h(0)
    stage_h(1)
    stage_y(last)
    stage_hs(0)
    stage_h(2)
    stage_hs(1)
    stage_ys(0)
    stage_ys(1)
    stage_scores(0)
    stage_hs(2)
    stage_scores(1)
    stage_h(last)
    stage_ys(2)
    stage_scores(2)
    stage_ys(last)
    stage_scores(last)

    def by_dest(core):
        return [(hh, xh, 4 * hh + 2 * core + xh) for hh in range(2) for xh in range(2)]

    f1_copies = [
        remote(
            scores.at[pl.ds(pl.multiple_of(4 * hh + 2 * (1 - c), 2), 2)], f1_in.at[hh],
            f1_s.at[hh], f1_r.at[hh], dev(dc=1),
        )
        for hh in range(2)
    ]
    for item in f1_copies:
        item.start()
    for item in f1_copies:
        item.wait_recv()
    for hh, xh, tile in by_dest(c):
        f1_acc[xh, hh] = scores[tile] + f1_in[hh, xh]

    f2_copies = []
    for dx in range(NX):
        for dy in range(NY):
            if dx or dy:
                n = dx * NY + dy - 1
                f2_copies.append(
                    remote(
                        f1_acc.at[((x + dx) % NX) // 2], f2_in.at[n],
                        f2_s.at[n], f2_r.at[n], dev(dx=dx, dy=dy),
                    )
                )
    for item in f2_copies:
        item.start()
    total = f1_acc[x // 2]
    for n, item in enumerate(f2_copies):
        item.wait_recv()
        total = total + f2_in[n]
    f2_acc[...] = total

    f3_copies = []
    for dh in range(NH):
        for dz in range(NZ):
            if dh or dz:
                n = dh * NZ + dz - 1
                tz = (z + dz) % NZ
                f3_copies.append(
                    remote(
                        f2_acc.at[(h + dh) % NH], f3_in.at[n],
                        f3_s.at[n], f3_r.at[n], dev(dh=dh, dz=tz - z),
                    )
                )
    for item in reversed(f3_copies):
        item.start()
    total = f2_acc[h]
    for n, item in enumerate(f3_copies):
        item.wait_recv()
        total = total + f3_in[n]
    lane = y * 32 + (x % 2) * 16 + z * 2
    moved = pltpu.roll(total, (slab - lane) % slab, 1)
    out[...] = moved.T[0:2, :]

    drain_gather()
    for k in range(CHUNKS):
        drain_chunk(k)
    for item in f1_copies + f2_copies + f3_copies:
        item.wait_send()


def per_device(activations, cotangents, gate_weight, down_weight, query_grads):
    rows, width = activations.shape
    hidden = gate_weight.shape[1]
    queries = query_grads.shape[0]
    slab = NX * rows
    part = slab // NY
    dma, vmem = pltpu.SemaphoreType.DMA, pltpu.VMEM
    n = CHUNKS
    scratch = [
        vmem((2, NZ, slab, width), BF16),
        vmem((hidden, width), BF16),
        vmem((hidden, width), BF16),
        vmem((queries, hidden, width), BF16),
        vmem((queries, width, hidden), BF16),
        vmem((n, width, 2 * slab), F32),
        vmem((n, 2, slab, hidden), BF16),
        vmem((n, 2, slab, hidden), BF16),
        vmem((n, 2, slab, hidden), F32),
        vmem((n, 2, slab, hidden), BF16),
        vmem((n, NY - 1, 2, part, hidden), BF16),
        vmem((n, 2, part, hidden), F32),
        vmem((n, 2, part, hidden), BF16),
        vmem((n, 2, part, hidden), BF16),
        vmem((n, 2, slab, hidden), BF16),
        vmem((NZ, queries, slab), F32),
        vmem((2, 2, queries, slab), F32),
        vmem((2, 2, queries, slab), F32),
        vmem((NX * NY - 1, 2, queries, slab), F32),
        vmem((2, queries, slab), F32),
        vmem((NH * NZ - 1, queries, slab), F32),
        dma((5,)),
        dma((2, NZ)), dma((2, NZ)),
        dma((2, 2 * NZ)), dma((2, 2 * NZ)),
        dma((2, 2 * NZ)), dma((2, 2 * NZ)),
        dma((n,)), dma((n,)),
        dma((n, NY - 1)), dma((n, NY - 1)),
        dma((n,)), dma((n,)),
        dma((n,)), dma((n,)),
        dma((n, NY - 1)), dma((n, NY - 1)),
        dma((n,)), dma((n,)),
        dma((2,)), dma((2,)),
        dma((NX * NY - 1,)), dma((NX * NY - 1,)),
        dma((NH * NZ - 1,)), dma((NH * NZ - 1,)),
    ]
    return pl.pallas_call(
        kernel,
        name="influence_scores",
        out_shape=jax.ShapeDtypeStruct((2, queries), F32),
        in_specs=[pl.BlockSpec(memory_space=pl.ANY)] * 5,
        out_specs=pl.BlockSpec(memory_space=pltpu.VMEM),
        scratch_shapes=scratch,
        cost_estimate=pl.CostEstimate(
            flops=2 * NZ * slab * width * hidden * (2 + queries),
            bytes_accessed=2 * width * hidden * (2 + queries),
            transcendentals=2 * part * hidden,
        ),
        compiler_params=pltpu.CompilerParams(
            collective_id=0, has_side_effects=True, vmem_limit_bytes=56 * 2**20
        ),
    )(activations, cotangents, gate_weight.T, down_weight, jnp.swapaxes(query_grads, 1, 2))


def solution(mesh):
    placed = (
        P("fsdp", "dp"),
        P("fsdp", "dp"),
        P("dp", "fsdp"),
        P("fsdp", "dp"),
        P(None, "dp", "fsdp"),
    )
    return jax.shard_map(
        per_device, mesh=mesh, in_specs=placed, out_specs=P(("dp", "fsdp"), None), check_vma=False
    )
```

time: 976 us -> 100 us (0.10)
  waiting for transfers between devices: 830 us -> 0 us
  blocking collectives: 111 us -> 0 us
  Pallas kernels: 0 us -> 98.5 us
  matrix products: 14.6 us -> 0 us
  between operations: 13.2 us -> 0.01 us
    all_gather x2 -> x0, waiting for transfers between devices: 427 us -> none  [the longest x1 220 us: per_device(): lax.all_gather(cotangents, 'fsdp', axis=0, tiled=True)]
    psum x1 -> x0, waiting for transfers between devices: 401 us -> none  [per_device(): gate_sum, back_sum = lax.psum((gate_partial, back_partial), 'dp')]
    unnamed x1 -> x0, blocking collectives: 111 us -> none
    pallas_call x0 -> x1, Pallas kernels: none -> 98.5 us  [per_device(): pl.pallas_call(kernel, name='influence_scores', out_shape=jax.ShapeDtypeS...]
    dot_general x4 -> x0, matrix products: 14.6 us -> none  [the longest x2 8.31 us: score_block(): jnp.einsum('ti,qij->tqj', act_rows, query_grads, preferred_element_type=j...]
  transfers between devices with their start and end apart: 3 -> 0, of which waited for: 3 -> 0; matrix products, arithmetic and copies ran while one was open for 0% -> 0% of each run, Pallas kernels for 0% -> 0%
where the time goes in v1:
time: 100 us; the launch traced here: 99.8 us
  Pallas kernels  98.5 us (98%)
  local copies, waits for them, and re-layouts  1.24 us (1%)
    pallas_call x1, Pallas kernels, per_device(): pl.pallas_call(kernel, name='influence_scores', out_shape=jax.ShapeDtypeS...  98.5 us

profile of v1, /device:TPU:1, one launch (start us, length us, event | category | flops | bytes accessed | tf_op | source)
XLA Modules:
  0.0 99.8 jit_solution(12856522337086630925)
XLA Ops:
  0.0 98.5 %influence_scores.1 = f32[2,8]{1,0:T(2,128)} custom-call(bf16[32,512]{1,0:T(8,128)(2,1)} %act.1, bf16[32,512]{1,0:T(8,128)(2,1)} %cot.1, bf16[448,512]{1,0:T(8,128)(2,1)} %bitcast.3, bf16[448,512]{1,0:T(8,128)(2,1)} %down_w.1, bf16[8,448,512]{2,1,0:T(8,128)(2,1)} %bitcast.2), custom_call_target="tpu_custom_call" | custom-call | flops 4697620480 | bytes 4587520 | tf_op jit(solution)/shard_map/influence_scores/pallas_call | solution.py:477
  98.5 1.2 %copy.7 = f32[2,8]{1,0:T(2,128)} copy(f32[2,8]{1,0:T(2,128)} %influence_scores.1) | data formatting | bytes 128

commit v2 on v1

--- a/solution.py
+++ b/solution.py
@@ -11,6 +11,7 @@
 F32 = jnp.float32
 BF16 = jnp.bfloat16
 NY, NH, NC, NX, NZ = 4, 2, 2, 4, 8
+REACH = 1
 CHUNKS = 4
 WHOLE_H = (False, False, False, True)
 
@@ -27,7 +28,7 @@
     ag, gw, dw, qt, qg, actt,
     c_out, c_in, acc, y_out, y_in, acc2, h_out, h_in, sig,
     scores, f1_in, f1_acc, f2_in, f2_acc, f3_in,
-    load, z_s, z_r, x_s, x_r, w_s, w_r,
+    told, load, z_s, z_r, x_s, x_r, w_s, w_r,
     c_s, c_r, y_s, y_r, h_s, h_r, hs_s, hs_r, ys_s, ys_r, cs_s, cs_r,
     f1_s, f1_r, f2_s, f2_r, f3_s, f3_r,
 ):
@@ -40,6 +41,10 @@
         tx, tz = (x + dx) % NX, z + dz
         return (ty * 4 + th * 2 + tc, tx * NZ + tz)
 
+    def ring(step):
+        at = (h * NZ + z + step + NH * NZ) % (NH * NZ)
+        return (y * 4 + (at // NZ) * 2 + c, x * NZ + at % NZ)
+
     rows, width = act.shape
     slab = NX * rows
     part, half = slab // NY, slab // NY // NH
@@ -51,7 +56,9 @@
         pltpu.make_async_copy(cot, ag.at[1, z, mine], load.at[1]),
         pltpu.make_async_copy(gate_w, gw, load.at[2]),
         pltpu.make_async_copy(down_w, dw, load.at[3]),
-        pltpu.make_async_copy(query, qt, load.at[4]),
+    ]
+    loads += [
+        pltpu.make_async_copy(query.at[q], qt.at[q], load.at[4 + q]) for q in range(queries)
     ]
     for item in loads:
         item.start()
@@ -63,16 +70,22 @@
 
     greet(dev(dx=1))
     greet(dev(dx=3))
-    pl.when(z > 0)(lambda: greet(dev(dz=-1)))
-    pl.when(z < NZ - 1)(lambda: greet(dev(dz=1)))
+    for near in range(1, max(REACH, 2) + 1):
+        greet(ring(near))
+        greet(ring(-near))
     greet(dev(dc=1))
     for dy in range(1, NY):
         greet(dev(dy=dy))
-    greet(dev(dh=1))
     loads[0].wait()
     loads[1].wait()
-    line = jnp.where(z > 0, 1, 0) + jnp.where(z < NZ - 1, 1, 0)
-    pl.semaphore_wait(barrier, line + 7)
+    pl.semaphore_wait(barrier, 6 + 2 * max(REACH, 2))
+
+    def tell(level, distance):
+        for device in (ring(distance), ring(-distance)):
+            pl.semaphore_signal(told.at[level], inc=1, device_id=device, device_id_type=MESH)
+
+    def hear(level):
+        pl.semaphore_wait(told.at[level], 2)
 
     def remote(src, dst, send, recv, device):
         return pltpu.make_async_remote_copy(
@@ -88,40 +101,48 @@
     def at_z(s, d):
         return jnp.clip(z - s if d == 0 else z + s, 0, NZ - 1)
 
-    def spot(zz, xx):
-        return (zz, pl.ds(pl.multiple_of(xx * rows, rows), rows))
-
-    def z_copy(s, d):
-        where = spot(at_z(s - 1, d), x)
-        block = ag.at[:, where[0], where[1]]
-        return remote(block, block, z_s.at[d, s], z_r.at[d, s], dev(dz=1 - 2 * d))
-
-    def z_land(s, d):
-        where = spot(at_z(s, d), x)
-        block = ag.at[:, where[0], where[1]]
-        return remote(block, block, z_s.at[d, s], z_r.at[d, s], dev(dz=2 * d - 1))
-
-    def x_copy(s, d, e):
-        where = spot(at_z(s, d), x)
-        block = ag.at[:, where[0], where[1]]
+    def piece(n, zz, xx):
+        return ag.at[n, zz, pl.ds(pl.multiple_of(xx * rows, rows), rows)]
+
+    def z_copy(s, d, n):
+        start = (s - 1) // REACH * REACH
+        block = piece(n, at_z(start, d), x)
+        step = (s - start) * (1 - 2 * d)
+        return remote(block, block, z_s.at[d, s, n], z_r.at[d, s, n], dev(dz=step))
+
+    def z_going(s, d):
+        start = (s - 1) // REACH * REACH
+        step = s - start
+        if d == 0:
+            return (z >= start) & (z + step <= NZ - 1)
+        return (z + start <= NZ - 1) & (z >= step)
+
+    def z_send(start, d, n):
+        if start % REACH == 0:
+            for s in range(min(start + REACH, NZ - 1), start, -1):
+                pl.when(z_going(s, d))(lambda s=s: z_copy(s, d, n).start())
+
+    def z_land(s, d, n):
+        block = piece(n, at_z(s, d), x)
+        return remote(block, block, z_s.at[d, s, n], z_r.at[d, s, n], dev(dz=2 * d - 1))
+
+    def x_copy(s, d, e, n):
+        block = piece(n, at_z(s, d), x)
         k = 2 * s + d
-        return remote(block, block, x_s.at[e, k], x_r.at[e, k], dev(dx=1 + 2 * e))
-
-    def x_land(s, d, e):
-        where = spot(at_z(s, d), (x + 3 - 2 * e) % NX)
-        block = ag.at[:, where[0], where[1]]
+        return remote(block, block, x_s.at[e, k, n], x_r.at[e, k, n], dev(dx=1 + 2 * e))
+
+    def x_land(s, d, e, n):
+        block = piece(n, at_z(s, d), (x + 3 - 2 * e) % NX)
         k = 2 * s + d
-        return remote(block, block, x_s.at[e, k], x_r.at[e, k], dev(dx=3 - 2 * e))
+        return remote(block, block, x_s.at[e, k, n], x_r.at[e, k, n], dev(dx=3 - 2 * e))
 
     def w_copy(s, d, e):
-        where = spot(at_z(s, d), (x + 3 - 2 * e) % NX)
-        block = ag.at[e, where[0], where[1]]
+        block = piece(e, at_z(s, d), (x + 3 - 2 * e) % NX)
         k = 2 * s + d
         return remote(block, block, w_s.at[e, k], w_r.at[e, k], dev(dx=1 + 2 * e))
 
     def w_land(s, d, e):
-        where = spot(at_z(s, d), (x + 2) % NX)
-        block = ag.at[e, where[0], where[1]]
+        block = piece(e, at_z(s, d), (x + 2) % NX)
         k = 2 * s + d
         return remote(block, block, w_s.at[e, k], w_r.at[e, k], dev(dx=3 - 2 * e))
 
@@ -131,23 +152,24 @@
     def step_z(s):
         for d in ds_of(s):
             def body(d=d):
-                if s:
-                    z_land(s, d).wait_recv()
-                if s < NZ - 1:
+                for n in range(2):
                     if s:
-                        pl.when(z < NZ - 1 if d == 0 else z > 0)(lambda: z_copy(s + 1, d).start())
+                        z_land(s, d, n).wait_recv()
+                        z_send(s, d, n)
                     else:
-                        pl.when(z < NZ - 1)(lambda: z_copy(1, 0).start())
-                        pl.when(z > 0)(lambda: z_copy(1, 1).start())
-                x_copy(s, d, 0).start()
-                x_copy(s, d, 1).start()
+                        z_send(0, 0, n)
+                        z_send(0, 1, n)
+                for n in range(2):
+                    x_copy(s, d, n, n).start()
+                for n in range(2):
+                    x_copy(s, d, 1 - n, n).start()
             pl.when(valid(s, d))(body)
 
     def step_x(s):
         for d in ds_of(s):
             def body(d=d):
                 for e in range(2):
-                    x_land(s, d, e).wait_recv()
+                    x_land(s, d, e, e).wait_recv()
                     w_copy(s, d, e).start()
             pl.when(valid(s, d))(body)
 
@@ -155,18 +177,22 @@
         for d in ds_of(s):
             def body(d=d):
                 for e in range(2):
+                    x_land(s, d, e, 1 - e).wait_recv()
                     w_land(s, d, e).wait_recv()
             pl.when(valid(s, d))(body)
 
     def drain_gather():
         for s, d in sides:
             if s:
-                going = (z >= s - 1) & (z < NZ - 1) if d == 0 else (z + s - 1 <= NZ - 1) & (z > 0)
-                pl.when(going)(lambda s=s, d=d: z_copy(s, d).wait_send())
+                def line_body(s=s, d=d):
+                    for n in range(2):
+                        z_copy(s, d, n).wait_send()
+                pl.when(z_going(s, d))(line_body)
 
             def body(s=s, d=d):
                 for e in range(2):
-                    x_copy(s, d, e).wait_send()
+                    for n in range(2):
+                        x_copy(s, d, e, n).wait_send()
                     w_copy(s, d, e).wait_send()
             pl.when(valid(s, d))(body)
 
@@ -309,7 +335,7 @@
             scores[second, pl.ds(q, 1), :] = line[:, slab:]
             return carry
 
-        lax.fori_loop(0, queries, one, 0)
+        lax.fori_loop(0, queries, one, 0, unroll=4)
 
     def drain_chunk(k):
         c_copy(k).wait_send()
@@ -329,8 +355,15 @@
         if step >= 2:
             step_w(step - 2)
         if step == 0:
-            loads[4].wait()
+            tell(0, 2)
+        elif step == 1:
+            hear(0)
+            tell(1, 4)
+        elif step == 4:
+            hear(1)
         if step < 4:
+            for q in (2 * step, 2 * step + 1):
+                loads[4 + q].wait()
             turn_queries(2 * step, 2)
         if step == 2:
             loads[2].wait()
@@ -346,23 +379,25 @@
                 stage_core(k)
             elif k >= 1:
                 stage_y(k - 1)
+        if step == 7:
+            stage_h(0)
+        elif step == 9:
+            stage_hs(0)
+            stage_h(1)
     last = CHUNKS - 1
     stage_core(last)
-    stage_h(0)
-    stage_h(1)
+    stage_ys(0)
     stage_y(last)
-    stage_hs(0)
+    stage_scores(0)
     stage_h(2)
     stage_hs(1)
-    stage_ys(0)
     stage_ys(1)
-    stage_scores(0)
-    stage_hs(2)
     stage_scores(1)
     stage_h(last)
+    stage_hs(2)
     stage_ys(2)
+    stage_ys(last)
     stage_scores(2)
-    stage_ys(last)
     stage_scores(last)
 
     def by_dest(core):
@@ -460,9 +495,10 @@
         vmem((NX * NY - 1, 2, queries, slab), F32),
         vmem((2, queries, slab), F32),
         vmem((NH * NZ - 1, queries, slab), F32),
-        dma((5,)),
-        dma((2, NZ)), dma((2, NZ)),
-        dma((2, 2 * NZ)), dma((2, 2 * NZ)),
+        pltpu.SemaphoreType.REGULAR((2,)),
+        dma((4 + queries,)),
+        dma((2, NZ, 2)), dma((2, NZ, 2)),
+        dma((2, 2 * NZ, 2)), dma((2, 2 * NZ, 2)),
         dma((2, 2 * NZ)), dma((2, 2 * NZ)),
         dma((n,)), dma((n,)),
         dma((n, NY - 1)), dma((n, NY - 1)),

time: 100 us -> 93.3 us (0.933)
  Pallas kernels: 98.5 us -> 91.6 us
    pallas_call x1, Pallas kernels: 98.5 us -> 91.6 us  [per_device(): pl.pallas_call(kernel, name='influence_scores', out_shape=jax.ShapeDtypeS...]
where the time goes in v2:
time: 93.3 us; the launch traced here: 92.9 us
  Pallas kernels  91.6 us (98%)
  local copies, waits for them, and re-layouts  1.24 us (1%)
    pallas_call x1, Pallas kernels, per_device(): pl.pallas_call(kernel, name='influence_scores', out_shape=jax.ShapeDtypeS...  91.6 us

profile of v2, /device:TPU:1, one launch (start us, length us, event | category | flops | bytes accessed | tf_op | source)
XLA Modules:
  0.0 92.9 jit_solution(7782953862890508356)
XLA Ops:
  0.0 91.6 %influence_scores.1 = f32[2,8]{1,0:T(2,128)} custom-call(bf16[32,512]{1,0:T(8,128)(2,1)} %act.1, bf16[32,512]{1,0:T(8,128)(2,1)} %cot.1, bf16[448,512]{1,0:T(8,128)(2,1)} %bitcast.3, bf16[448,512]{1,0:T(8,128)(2,1)} %down_w.1, bf16[8,448,512]{2,1,0:T(8,128)(2,1)} %bitcast.2), custom_call_target="tpu_custom_call" | custom-call | flops 4697620480 | bytes 4587520 | tf_op jit(solution)/shard_map/influence_scores/pallas_call | solution.py:513
  91.6 1.2 %copy.7 = f32[2,8]{1,0:T(2,128)} copy(f32[2,8]{1,0:T(2,128)} %influence_scores.1) | data formatting | bytes 128

commit v3 on v2

--- a/solution.py
+++ b/solution.py
@@ -104,11 +104,14 @@
     def piece(n, zz, xx):
         return ag.at[n, zz, pl.ds(pl.multiple_of(xx * rows, rows), rows)]
 
+    def both(zz, xx):
+        return ag.at[:, zz, pl.ds(pl.multiple_of(xx * rows, rows), rows)]
+
     def z_copy(s, d, n):
         start = (s - 1) // REACH * REACH
-        block = piece(n, at_z(start, d), x)
+        block = both(at_z(start, d), x)
         step = (s - start) * (1 - 2 * d)
-        return remote(block, block, z_s.at[d, s, n], z_r.at[d, s, n], dev(dz=step))
+        return remote(block, block, z_s.at[d, s, 0], z_r.at[d, s, 0], dev(dz=step))
 
     def z_going(s, d):
         start = (s - 1) // REACH * REACH
@@ -123,8 +126,8 @@
                 pl.when(z_going(s, d))(lambda s=s: z_copy(s, d, n).start())
 
     def z_land(s, d, n):
-        block = piece(n, at_z(s, d), x)
-        return remote(block, block, z_s.at[d, s, n], z_r.at[d, s, n], dev(dz=2 * d - 1))
+        block = both(at_z(s, d), x)
+        return remote(block, block, z_s.at[d, s, 0], z_r.at[d, s, 0], dev(dz=2 * d - 1))
 
     def x_copy(s, d, e, n):
         block = piece(n, at_z(s, d), x)
@@ -152,13 +155,12 @@
     def step_z(s):
         for d in ds_of(s):
             def body(d=d):
-                for n in range(2):
-                    if s:
-                        z_land(s, d, n).wait_recv()
-                        z_send(s, d, n)
-                    else:
-                        z_send(0, 0, n)
-                        z_send(0, 1, n)
+                if s:
+                    z_land(s, d, 0).wait_recv()
+                    z_send(s, d, 0)
+                else:
+                    z_send(0, 0, 0)
+                    z_send(0, 1, 0)
                 for n in range(2):
                     x_copy(s, d, n, n).start()
                 for n in range(2):
@@ -185,8 +187,7 @@
         for s, d in sides:
             if s:
                 def line_body(s=s, d=d):
-                    for n in range(2):
-                        z_copy(s, d, n).wait_send()
+                    z_copy(s, d, 0).wait_send()
                 pl.when(z_going(s, d))(line_body)
 
             def body(s=s, d=d):
@@ -391,10 +392,10 @@
     stage_scores(0)
     stage_h(2)
     stage_hs(1)
+    stage_h(last)
+    stage_hs(2)
     stage_ys(1)
     stage_scores(1)
-    stage_h(last)
-    stage_hs(2)
     stage_ys(2)
     stage_ys(last)
     stage_scores(2)
@@ -428,8 +429,11 @@
                         f2_s.at[n], f2_r.at[n], dev(dx=dx, dy=dy),
                     )
                 )
-    for item in f2_copies:
-        item.start()
+    for dx, dy in sorted(
+        ((dx, dy) for dx in range(NX) for dy in range(NY) if dx or dy),
+        key=lambda to: -min(to[0], NX - to[0]) - min(to[1], NY - to[1]),
+    ):
+        f2_copies[dx * NY + dy - 1].start()
     total = f1_acc[x // 2]
     for n, item in enumerate(f2_copies):
         item.wait_recv()
@@ -448,8 +452,8 @@
                         f3_s.at[n], f3_r.at[n], dev(dh=dh, dz=tz - z),
                     )
                 )
-    for item in reversed(f3_copies):
-        item.start()
+    for n in (*range(NZ - 1, NH * NZ - 1), *range(NZ - 2, -1, -1)):
+        f3_copies[n].start()
     total = f2_acc[h]
     for n, item in enumerate(f3_copies):
         item.wait_recv()

time: 93.3 us -> 92.5 us (level)
  Pallas kernels: 91.6 us -> 90.4 us
    pallas_call x1, Pallas kernels: 91.6 us -> 90.4 us  [per_device(): pl.pallas_call(kernel, name='influence_scores', out_shape=jax.ShapeDtypeS...]
where the time goes in v3:
time: 92.5 us; the launch traced here: 91.6 us
  Pallas kernels  90.4 us (98%)
  local copies, waits for them, and re-layouts  1.24 us (1%)
    pallas_call x1, Pallas kernels, per_device(): pl.pallas_call(kernel, name='influence_scores', out_shape=jax.ShapeDtypeS...  90.4 us

profile of v3, /device:TPU:1, one launch (start us, length us, event | category | flops | bytes accessed | tf_op | source)
XLA Modules:
  0.0 91.6 jit_solution(16447460407867138218)
XLA Ops:
  0.0 90.4 %influence_scores.1 = f32[2,8]{1,0:T(2,128)} custom-call(bf16[32,512]{1,0:T(8,128)(2,1)} %act.1, bf16[32,512]{1,0:T(8,128)(2,1)} %cot.1, bf16[448,512]{1,0:T(8,128)(2,1)} %bitcast.3, bf16[448,512]{1,0:T(8,128)(2,1)} %down_w.1, bf16[8,448,512]{2,1,0:T(8,128)(2,1)} %bitcast.2), custom_call_target="tpu_custom_call" | custom-call | flops 4697620480 | bytes 4587520 | tf_op jit(solution)/shard_map/influence_scores/pallas_call | solution.py:517
  90.4 1.2 %copy.7 = f32[2,8]{1,0:T(2,128)} copy(f32[2,8]{1,0:T(2,128)} %influence_scores.1) | data formatting | bytes 128
